TPU v7x, 32 devices: a whole 2x2x4 slice. The times are simulated.
32 devices in a mesh: pair: 8 (over z, y), rad: 4 (over x, core).
Axes of the slice: x: 2, y: 2, z: 4, core: 2. Of those that a mesh axis runs over, the one named last changes fastest.
Arguments:
- orbitals: bfloat16 [500, 1024], replicated, may hold values from -6 to 6
- kernel: bfloat16 [12, 1024, 1024], P(None, 'rad', 'pair'), may hold values from -0.1875 to 0.1875
- bessel: bfloat16 [12, 128, 1024], replicated, may hold values from -1.5 to 1.5
- angular: float32 [32, 12, 16], P(('pair', 'rad')), may hold values from -6 to 6
- state_l: int32 [500], replicated, may hold values from 0 to 6
- tile_blocks: int32 [32, 2], replicated, may hold values from 0 to 124, as said below
Outputs:
- upper: bfloat16 [32, 512, 512], P(('pair', 'rad'))
- lower: bfloat16 [32, 512, 512], P(('pair', 'rad'))
Inputs may be any that keep to these rules, and one draw needn't show every extreme that they name: `tile_blocks`: each row names a tile by its row and column state block, the first not above the second; no tile appears twice.
All inputs are finite; a program needn't handle non-finite values.
Results may differ from a plain program's by a relative error of at most 0.0065.
Values may be sent and summed in bfloat16 or wider, within the bound.
A program may use at most 128 MiB of HBM per device.

v0:
```python
import jax
import jax.numpy as jnp
from jax import lax
from jax.sharding import PartitionSpec as P

NL = 12
SB = 4


def from_partner(block, axis, apart):
    count = lax.axis_size(axis)
    route = []
    for low in range(count):
        high = low | 1 << apart
        if high != low and high < count:
            route += [(low, high), (high, low)]
    return lax.ppermute(block, axis, route)


def tile_states(blocks):
    offsets = jnp.arange(SB, dtype=jnp.int32)
    row_states = blocks[:, 0:1] * SB + offsets[None, :]
    col_states = blocks[:, 1:2] * SB + offsets[None, :]
    return (row_states, col_states)


def selection_mask(state_l, row_states, col_states):
    left_l = state_l[row_states][:, :, None]
    right_l = state_l[col_states][:, None, :]
    orders = jnp.arange(NL, dtype=jnp.int32)[None, :, None, None]
    low_end = jnp.abs(left_l - right_l)[:, None]
    high_end = (left_l + right_l)[:, None]
    parity = (high_end + orders) % 2 == 0
    allowed = (orders >= low_end) & (orders <= high_end) & parity
    return allowed.astype(jnp.int32)


def build_density(orbitals, row_states, col_states):
    left_orb = orbitals[row_states].astype(jnp.float32)
    right_orb = orbitals[col_states].astype(jnp.float32)
    product = left_orb[:, :, None, :] * right_orb[:, None, :, :]
    return product.reshape(product.shape[0], SB * SB, product.shape[-1]).astype(jnp.bfloat16)


def body(orbitals, kernel, bessel, angular, state_l, tile_blocks):
    pair_count = lax.axis_size("pair")
    rad_count = lax.axis_size("rad")
    pair_index = lax.axis_index("pair")
    rad_index = lax.axis_index("rad")
    owner_tiles = tile_blocks.shape[0] // pair_count
    radial_total = orbitals.shape[1]
    order_count = kernel.shape[0]
    momenta = bessel.shape[1]
    own_blocks = lax.dynamic_slice_in_dim(tile_blocks, pair_index * owner_tiles, owner_tiles, 0)
    row_states, col_states = tile_states(own_blocks)
    density = build_density(orbitals, row_states, col_states)
    form_sum = jnp.einsum(
        "lrq,teq->tler",
        lax.all_gather(kernel, "pair", axis=2, tiled=True),
        density,
        preferred_element_type=jnp.float32,
    )
    form_local = form_sum.astype(jnp.bfloat16)
    form_owned = lax.all_to_all(form_local, "rad", split_axis=0, concat_axis=3, tiled=True)
    member_count = form_owned.shape[0]
    first_tile = (pair_index * rad_count + rad_index) * member_count
    mine = lax.dynamic_slice_in_dim(tile_blocks, first_tile, member_count, 0)
    row_states, col_states = tile_states(mine)
    allowed = selection_mask(state_l, row_states, col_states)
    weights = angular.reshape(member_count, order_count, SB, SB) * allowed.astype(jnp.float32)

    def order_term(form_tile, weight_tile, order):
        form_layer = lax.dynamic_index_in_dim(form_tile, order, 0, keepdims=False).reshape(
            SB, SB, radial_total
        )
        factor = lax.dynamic_index_in_dim(weight_tile, order, 0, keepdims=False)
        radial = lax.dynamic_index_in_dim(bessel, order, 0, keepdims=False)
        scaled = (factor[:, :, None] * form_layer.astype(jnp.float32))[
            :, :, None, :
        ] * radial.astype(jnp.float32)[None, None, :, :]
        scaled = scaled.astype(jnp.bfloat16)
        product = jnp.einsum("sukr,qr->skuq", scaled, radial, preferred_element_type=jnp.float32)
        return product.reshape(SB * momenta, SB * momenta)

    form_tile = form_owned[0]
    weight_tile = weights[0]

    def order_step(order, accum):
        return accum + order_term(form_tile, weight_tile, order)

    initial_sum = jnp.zeros((SB * momenta, SB * momenta), jnp.float32)
    accum = lax.fori_loop(0, order_count, order_step, initial_sum)
    results = [accum]
    upper = jnp.stack(results).astype(jnp.bfloat16)
    top_bit = pair_count.bit_length() - 2
    partner = from_partner(upper, "pair", top_bit)
    lower = jnp.transpose(partner, (0, 2, 1))
    return (upper, lower)


def solution(mesh):
    in_specs = (P(), P(None, "rad", "pair"), P(), P(("pair", "rad"), None, None), P(), P())
    out_specs = (P(("pair", "rad"), None, None), P(("pair", "rad"), None, None))
    return jax.shard_map(body, mesh=mesh, in_specs=in_specs, out_specs=out_specs, check_vma=False)
```

profile of v0, /device:TPU:0, one launch (start us, length us, event | category | flops | bytes accessed | tf_op | source)
XLA Modules:
  0.0 240.8 jit_solution(2937949747011470248)
XLA Ops:
  7.2 0.7 all-gather.2.cloned.1.call-update
  7.9 0.8 constant_dynamic-slice_fusion.1
  8.7 0.5 fusion.22
  10.5 1.3 gather_fusion
  11.8 1.3 gather_fusion.1
  13.2 0.8 constant_dynamic-slice_fusion
  14.1 0.6 gather_fusion.2
  14.8 0.6 gather_fusion.3
  15.6 97.2 %all-gather.2.cloned.1.call-done = bf16[12,256,1024]{2,1,0:T(8,128)(2,1)} async-done(((bf16[12,256,128]{2,1,0:T(8,128)(2,1)}), bf16[12,256,1024]{2,1,0:T(8,128)(2,1)}) %all-gather.2.cloned.1.call-update) | async-done | bytes 6291472 | tf_op jit(solution)/shard_map/all_gather | solution.py:59
  112.7 5.6 %fusion.12 = bf16[4,12,16,256]{3,2,1,0:T(8,128)(2,1)} fusion(bf16[12,256,1024]{2,1,0:T(8,128)(2,1)} %all-gather.2.cloned.1.call-done, bf16[4,16,1024,1]{2,1,0,3:T(8,128)(2,1)S(1)} %reshape.327), kind=kOutput, calls=%fused_computation.20 | convolution fusion | flops 402849792 | bytes 6815744 | tf_op jit(solution)/shard_map/lrq,teq->tler/dot_general | solution.py:57
  118.3 3.5 %all-to-all-start = ((bf16[4,12,16,256]{3,2,1,0:T(8,128)(2,1)}), bf16[4,12,16,256]{3,2,1,0:T(8,128)(2,1)S(1)}, u32[]{:S(2)}, u32[]{:S(2)}) async-start(bf16[4,12,16,256]{3,2,1,0:T(8,128)(2,1)} %fusion.12), calls=%async_computation | async-start | bytes 786432 | tf_op jit(solution)/shard_map/all_to_all | solution.py:64
  122.1 7.0 %all-to-all-done = bf16[4,12,16,256]{3,2,1,0:T(8,128)(2,1)S(1)} async-done(((bf16[4,12,16,256]{3,2,1,0:T(8,128)(2,1)}), bf16[4,12,16,256]{3,2,1,0:T(8,128)(2,1)S(1)}, u32[]{:S(2)}, u32[]{:S(2)}) %all-to-all-start) | async-done | bytes 393248 | tf_op jit(solution)/shard_map/all_to_all | solution.py:64
  129.2 0.3 copy.11
  129.7 78.3 %while.14 = (s32[]{:T(128)}, f32[512,512]{1,0:T(8,128)S(1)}, bf16[12,128,1024]{2,1,0:T(8,128)(2,1)}, f32[12,4,4]{2,1,0:T(4,128)S(1)}, bf16[12,16,1024]{2,1,0:T(8,128)(2,1)S(1)}, /*index=5*/s32[]{:T(128)}, s32[]{:T(128)}) while((s32[]{:T(128)}, f32[512,512]{1,0:T(8,128)S(1)}, bf16[12,128,1024]{2,1,0:T(8,128)(2,1)}, ...), condition=%wide.region_1.2_spmd.clone, body=%wide.region_0.1_spmd.clone.sunk | while | flops 541753344 | bytes 8291107 | solution.py:92
  129.9 1.0 bitcast_convert_fusion.2
  130.9 3.4 %fusion.26 = f32[4,128,4,128]{1,3,2,0:T(8,128)} fusion(f32[128,1024]{1,0:T(8,128)S(1)} %bitcast_convert_fusion.2, f32[4,4,1024]{2,1,0:T(4,128)S(1)} %broadcast_multiply_fusion.2, bf16[12,128,1024]{2,1,0:T(8,128)(2,1)} %get-tuple-element.187, s32[]{:T(128)} %get-tuple-element.178), kind=kOutput, calls=%fused_computation.8.clone.1 | convolution fusion | flops 541065216 | bytes 1901056 | tf_op jit(solution)/shard_map/while/body/eval_jaxpr/sukr,qr->skuq/dot_general | solution.py:82
  134.4 1.6 copy.21
  136.0 0.3 bitcast_add_fusion.2
  136.4 1.0 bitcast_convert_fusion.2
  137.4 3.4 %fusion.26 = f32[4,128,4,128]{1,3,2,0:T(8,128)} fusion(f32[128,1024]{1,0:T(8,128)S(1)} %bitcast_convert_fusion.2, f32[4,4,1024]{2,1,0:T(4,128)S(1)} %broadcast_multiply_fusion.2, bf16[12,128,1024]{2,1,0:T(8,128)(2,1)} %get-tuple-element.187, s32[]{:T(128)} %get-tuple-element.178), kind=kOutput, calls=%fused_computation.8.clone.1 | convolution fusion | flops 541065216 | bytes 1901056 | tf_op jit(solution)/shard_map/while/body/eval_jaxpr/sukr,qr->skuq/dot_general | solution.py:82
  140.9 1.6 copy.21
  142.5 0.3 bitcast_add_fusion.2
  143.0 1.0 bitcast_convert_fusion.2
  144.0 3.4 %fusion.26 = f32[4,128,4,128]{1,3,2,0:T(8,128)} fusion(f32[128,1024]{1,0:T(8,128)S(1)} %bitcast_convert_fusion.2, f32[4,4,1024]{2,1,0:T(4,128)S(1)} %broadcast_multiply_fusion.2, bf16[12,128,1024]{2,1,0:T(8,128)(2,1)} %get-tuple-element.187, s32[]{:T(128)} %get-tuple-element.178), kind=kOutput, calls=%fused_computation.8.clone.1 | convolution fusion | flops 541065216 | bytes 1901056 | tf_op jit(solution)/shard_map/while/body/eval_jaxpr/sukr,qr->skuq/dot_general | solution.py:82
  147.4 1.6 copy.21
  149.0 0.3 bitcast_add_fusion.2
  149.5 1.0 bitcast_convert_fusion.2
  150.5 3.4 %fusion.26 = f32[4,128,4,128]{1,3,2,0:T(8,128)} fusion(f32[128,1024]{1,0:T(8,128)S(1)} %bitcast_convert_fusion.2, f32[4,4,1024]{2,1,0:T(4,128)S(1)} %broadcast_multiply_fusion.2, bf16[12,128,1024]{2,1,0:T(8,128)(2,1)} %get-tuple-element.187, s32[]{:T(128)} %get-tuple-element.178), kind=kOutput, calls=%fused_computation.8.clone.1 | convolution fusion | flops 541065216 | bytes 1901056 | tf_op jit(solution)/shard_map/while/body/eval_jaxpr/sukr,qr->skuq/dot_general | solution.py:82
  153.9 1.6 copy.21
  155.6 0.3 bitcast_add_fusion.2
  156.0 1.0 bitcast_convert_fusion.2
  157.0 3.4 %fusion.26 = f32[4,128,4,128]{1,3,2,0:T(8,128)} fusion(f32[128,1024]{1,0:T(8,128)S(1)} %bitcast_convert_fusion.2, f32[4,4,1024]{2,1,0:T(4,128)S(1)} %broadcast_multiply_fusion.2, bf16[12,128,1024]{2,1,0:T(8,128)(2,1)} %get-tuple-element.187, s32[]{:T(128)} %get-tuple-element.178), kind=kOutput, calls=%fused_computation.8.clone.1 | convolution fusion | flops 541065216 | bytes 1901056 | tf_op jit(solution)/shard_map/while/body/eval_jaxpr/sukr,qr->skuq/dot_general | solution.py:82
  160.5 1.6 copy.21
  162.1 0.3 bitcast_add_fusion.2
  162.5 1.0 bitcast_convert_fusion.2
  163.5 3.4 %fusion.26 = f32[4,128,4,128]{1,3,2,0:T(8,128)} fusion(f32[128,1024]{1,0:T(8,128)S(1)} %bitcast_convert_fusion.2, f32[4,4,1024]{2,1,0:T(4,128)S(1)} %broadcast_multiply_fusion.2, bf16[12,128,1024]{2,1,0:T(8,128)(2,1)} %get-tuple-element.187, s32[]{:T(128)} %get-tuple-element.178), kind=kOutput, calls=%fused_computation.8.clone.1 | convolution fusion | flops 541065216 | bytes 1901056 | tf_op jit(solution)/shard_map/while/body/eval_jaxpr/sukr,qr->skuq/dot_general | solution.py:82
  167.0 1.6 copy.21
  168.6 0.3 bitcast_add_fusion.2
  169.1 1.0 bitcast_convert_fusion.2
  170.1 3.4 %fusion.26 = f32[4,128,4,128]{1,3,2,0:T(8,128)} fusion(f32[128,1024]{1,0:T(8,128)S(1)} %bitcast_convert_fusion.2, f32[4,4,1024]{2,1,0:T(4,128)S(1)} %broadcast_multiply_fusion.2, bf16[12,128,1024]{2,1,0:T(8,128)(2,1)} %get-tuple-element.187, s32[]{:T(128)} %get-tuple-element.178), kind=kOutput, calls=%fused_computation.8.clone.1 | convolution fusion | flops 541065216 | bytes 1901056 | tf_op jit(solution)/shard_map/while/body/eval_jaxpr/sukr,qr->skuq/dot_general | solution.py:82
  173.5 1.6 copy.21
  175.1 0.3 bitcast_add_fusion.2
  175.6 1.0 bitcast_convert_fusion.2
  176.6 3.4 %fusion.26 = f32[4,128,4,128]{1,3,2,0:T(8,128)} fusion(f32[128,1024]{1,0:T(8,128)S(1)} %bitcast_convert_fusion.2, f32[4,4,1024]{2,1,0:T(4,128)S(1)} %broadcast_multiply_fusion.2, bf16[12,128,1024]{2,1,0:T(8,128)(2,1)} %get-tuple-element.187, s32[]{:T(128)} %get-tuple-element.178), kind=kOutput, calls=%fused_computation.8.clone.1 | convolution fusion | flops 541065216 | bytes 1901056 | tf_op jit(solution)/shard_map/while/body/eval_jaxpr/sukr,qr->skuq/dot_general | solution.py:82
  180.0 1.6 copy.21
  181.7 0.3 bitcast_add_fusion.2
  182.1 1.0 bitcast_convert_fusion.2
  183.1 3.4 %fusion.26 = f32[4,128,4,128]{1,3,2,0:T(8,128)} fusion(f32[128,1024]{1,0:T(8,128)S(1)} %bitcast_convert_fusion.2, f32[4,4,1024]{2,1,0:T(4,128)S(1)} %broadcast_multiply_fusion.2, bf16[12,128,1024]{2,1,0:T(8,128)(2,1)} %get-tuple-element.187, s32[]{:T(128)} %get-tuple-element.178), kind=kOutput, calls=%fused_computation.8.clone.1 | convolution fusion | flops 541065216 | bytes 1901056 | tf_op jit(solution)/shard_map/while/body/eval_jaxpr/sukr,qr->skuq/dot_general | solution.py:82
  186.6 1.6 copy.21
  188.2 0.3 bitcast_add_fusion.2
  188.6 1.0 bitcast_convert_fusion.2
  189.7 3.4 %fusion.26 = f32[4,128,4,128]{1,3,2,0:T(8,128)} fusion(f32[128,1024]{1,0:T(8,128)S(1)} %bitcast_convert_fusion.2, f32[4,4,1024]{2,1,0:T(4,128)S(1)} %broadcast_multiply_fusion.2, bf16[12,128,1024]{2,1,0:T(8,128)(2,1)} %get-tuple-element.187, s32[]{:T(128)} %get-tuple-element.178), kind=kOutput, calls=%fused_computation.8.clone.1 | convolution fusion | flops 541065216 | bytes 1901056 | tf_op jit(solution)/shard_map/while/body/eval_jaxpr/sukr,qr->skuq/dot_general | solution.py:82
  193.1 1.6 copy.21
  194.7 0.3 bitcast_add_fusion.2
  195.2 1.0 bitcast_convert_fusion.2
  196.2 3.4 %fusion.26 = f32[4,128,4,128]{1,3,2,0:T(8,128)} fusion(f32[128,1024]{1,0:T(8,128)S(1)} %bitcast_convert_fusion.2, f32[4,4,1024]{2,1,0:T(4,128)S(1)} %broadcast_multiply_fusion.2, bf16[12,128,1024]{2,1,0:T(8,128)(2,1)} %get-tuple-element.187, s32[]{:T(128)} %get-tuple-element.178), kind=kOutput, calls=%fused_computation.8.clone.1 | convolution fusion | flops 541065216 | bytes 1901056 | tf_op jit(solution)/shard_map/while/body/eval_jaxpr/sukr,qr->skuq/dot_general | solution.py:82
  199.6 1.6 copy.21
  201.3 0.3 bitcast_add_fusion.2
  201.7 1.0 bitcast_convert_fusion.2
  202.7 3.4 %fusion.26 = f32[4,128,4,128]{1,3,2,0:T(8,128)} fusion(f32[128,1024]{1,0:T(8,128)S(1)} %bitcast_convert_fusion.2, f32[4,4,1024]{2,1,0:T(4,128)S(1)} %broadcast_multiply_fusion.2, bf16[12,128,1024]{2,1,0:T(8,128)(2,1)} %get-tuple-element.187, s32[]{:T(128)} %get-tuple-element.178), kind=kOutput, calls=%fused_computation.8.clone.1 | convolution fusion | flops 541065216 | bytes 1901056 | tf_op jit(solution)/shard_map/while/body/eval_jaxpr/sukr,qr->skuq/dot_general | solution.py:82
  206.1 1.6 copy.21
  208.4 1.6 collective-permute-start
  210.0 23.2 %collective-permute-done = bf16[1,512,512]{1,2,0:T(8,128)(2,1)S(1)} collective-permute-done((bf16[1,512,512]{1,2,0:T(8,128)(2,1)S(1)}, bf16[1,512,512]{1,2,0:T(8,128)(2,1)S(1)}, u32[]{:S(2)}, u32[]{:S(2)}) %collective-permute-start) | collective-permute-done | bytes 524320 | tf_op jit(solution)/shard_map/ppermute | solution.py:17
  233.1 0.8 copy.29
  (77 shorter events, 3.2 us)
Async XLA Ops:
  7.2 6.9 %copy-start = (bf16[500,1024]{1,0:T(8,128)(2,1)S(1)}, bf16[500,1024]{1,0:T(8,128)(2,1)}, u32[]{:S(2)}) copy-start(bf16[500,1024]{1,0:T(8,128)(2,1)} %param.8) | copy-start | bytes 3072004
  7.2 105.5 %all-gather.2.cloned.1.call-start = ((), (), s32[]{:S(2)}) async-start(), calls=%async_computation.1 | async-start | bytes 7077888 | tf_op jit(solution)/shard_map/all_gather | solution.py:59
  15.5 106.3 %copy-start.2 = (f32[1,12,16]{2,0,1:T(1,128)S(1)}, f32[1,12,16]{2,0,1:T(1,128)}, u32[]{:S(2)}) copy-start(f32[1,12,16]{2,0,1:T(1,128)} %param.11) | copy-start | bytes 2308
  118.3 10.9 %all-to-all-start = ((bf16[4,12,16,256]{3,2,1,0:T(8,128)(2,1)}), bf16[4,12,16,256]{3,2,1,0:T(8,128)(2,1)S(1)}, u32[]{:S(2)}, u32[]{:S(2)}) async-start(bf16[4,12,16,256]{3,2,1,0:T(8,128)(2,1)} %fusion.12), calls=%async_computation | async-start | bytes 786432 | tf_op jit(solution)/shard_map/all_to_all | solution.py:64
  208.1 25.8 %copy-start.1 = (bf16[1,512,512]{2,1,0:T(8,128)(2,1)}, bf16[1,512,512]{2,1,0:T(8,128)(2,1)S(1)}, u32[]{:S(2)}) copy-start(bf16[1,512,512]{2,1,0:T(8,128)(2,1)S(1)} %convert_bitcast_fusion) | copy-start | bytes 1572868
  208.4 24.7 %collective-permute-start = (bf16[1,512,512]{1,2,0:T(8,128)(2,1)S(1)}, bf16[1,512,512]{1,2,0:T(8,128)(2,1)S(1)}, u32[]{:S(2)}, u32[]{:S(2)}) collective-permute-start(bf16[1,512,512]{1,2,0:T(8,128)(2,1)S(1)} %copy.13), channel_id=1, source_target_pairs={{0,16},{16,0},{4,20},{20,4},{8,24},{24,8},{12,28},{28,12},{1,17},{... | collective-permute-start | bytes 1572872 | tf_op jit(solution)/shard_map/ppermute | solution.py:17
Sparse Core Ops, SparseCore 0:
  10.1 102.6 all-gather.1
where the time goes:
time: 242 us; the launch traced here: 241 us
  waiting for transfers between devices  128 us (53%)
  matrix products  46.9 us (19%)
  local copies, waits for them, and re-layouts  27.8 us (11%)
  other arithmetic  16.8 us (7%)
  between operations  15.4 us (6%)
  starting transfers between devices  5.08 us (2%)
    all_gather x1, waiting for transfers between devices, body(): lax.all_gather(kernel, 'pair', axis=2, tiled=True)  97.2 us
    dot_general x12, matrix products, order_term(): jnp.einsum('sukr,qr->skuq', scaled, radial, preferred_element_type=jnp.fl...  41.3 us
    ppermute x1, waiting for transfers between devices, from_partner(): return lax.ppermute(block, axis, route)  23.2 us
    transpose x12, local copies, waits for them, and re-layouts, order_term(): jnp.einsum('sukr,qr->skuq', scaled, radial, preferred_element_type=jnp.fl...  19.4 us
    convert_element_type x12, other arithmetic, order_term(): radial.astype(jnp.float32)[None, None, :, :]  11.9 us
    all_to_all x1, waiting for transfers between devices, body(): lax.all_to_all(form_local, 'rad', split_axis=0, concat_axis=3, tiled=True)  7.05 us
    dot_general x1, matrix products, body(): jnp.einsum('lrq,teq->tler', lax.all_gather(kernel, 'pair', axis=2, tiled=...  5.56 us
  transfers between devices with their start and end apart: 3, of which 3 were waited for; matrix products, arithmetic and copies ran while one was open for 3% of the time, Pallas kernels for 0%

commit v1 on v0

v1 whole, which is shorter than its diff:
```python
import functools

import jax
import jax.numpy as jnp
from jax import lax
from jax.experimental import pallas as pl
from jax.experimental.pallas import tpu as pltpu
from jax.sharding import PartitionSpec as P

SB = 4
PAIRS = SB * SB
CHUNK = 2
NT_DIMS = (((1,), (1,)), ((), ()))


def partial_form_kernel(rows_ref, cols_ref, l_ref, orb_ref, kernel_ref, out_ref):
    groups, members, slots = out_ref.shape[:3]
    count = rows_ref.shape[0]
    states = orb_ref.shape[0]
    ids = lax.broadcasted_iota(jnp.int32, (count, states), 1)
    left_hot = ids == rows_ref[...]
    right_hot = ids == cols_ref[...]
    levels = l_ref[...].astype(jnp.float32)

    def pick(hot):
        value = jnp.dot(
            jnp.where(hot, 1.0, 0.0).astype(jnp.bfloat16), orb_ref[...], preferred_element_type=jnp.float32
        )
        level = jnp.sum(jnp.where(hot, levels, 0.0), axis=1, keepdims=True)
        return value, level

    left, left_l = pick(left_hot)
    right, right_l = pick(right_hot)
    density = (left * right).astype(jnp.bfloat16)
    odd = ((left_l + right_l).astype(jnp.int32) & 1) == 1
    for slot in range(slots):
        even_form = lax.dot_general(density, kernel_ref[2 * slot], NT_DIMS, preferred_element_type=jnp.float32)
        odd_form = lax.dot_general(density, kernel_ref[2 * slot + 1], NT_DIMS, preferred_element_type=jnp.float32)
        form = jnp.where(odd, odd_form, even_form).astype(jnp.bfloat16)
        form = form.reshape(groups, members, PAIRS, form.shape[-1])
        for group in range(groups):
            for member in range(members):
                out_ref[group, member, slot] = form[group, member]


def partial_form(orbitals, kernel, state_l, tile_blocks, pair_count, rad_count):
    tiles = tile_blocks.shape[0]
    states = orbitals.shape[0]
    orders, radial, depth = kernel.shape
    place = jnp.arange(PAIRS, dtype=jnp.int32)[None]
    rows = (tile_blocks[:, 0:1] * SB + place // SB).reshape(tiles * PAIRS, 1)
    cols = (tile_blocks[:, 1:2] * SB + place % SB).reshape(tiles * PAIRS, 1)
    members = tiles // pair_count
    groups = 2
    block = groups * members * PAIRS
    return pl.pallas_call(
        partial_form_kernel,
        grid=(pair_count // groups,),
        out_shape=jax.ShapeDtypeStruct((pair_count, members, orders // 2, PAIRS, radial), jnp.bfloat16),
        in_specs=[
            pl.BlockSpec((block, 1), lambda i: (i, 0)),
            pl.BlockSpec((block, 1), lambda i: (i, 0)),
            pl.BlockSpec((1, states), lambda i: (0, 0)),
            pl.BlockSpec((states, depth), lambda i: (0, lax.axis_index("pair"))),
            pl.BlockSpec((orders, radial, depth), lambda i: (0, 0, 0)),
        ],
        out_specs=pl.BlockSpec((groups, members, orders // 2, PAIRS, radial), lambda i: (i, 0, 0, 0, 0)),
        compiler_params=pltpu.CompilerParams(vmem_limit_bytes=32 * 2**20),
        cost_estimate=pl.CostEstimate(
            flops=2 * tiles * PAIRS * orders * radial * depth, bytes_accessed=4 * 2**20, transcendentals=0
        ),
        name="partial_form",
    )(rows, cols, state_l.reshape(1, states), orbitals, kernel)


def block_kernel(flip, tile_ref, tiles_ref, l_ref, angular_ref, form_ref, bessel_ref, out_ref):
    parts, slots = form_ref.shape[:2]
    orders, momenta = bessel_ref.shape[:2]
    tile = tile_ref[0]
    row_block = tiles_ref[tile, 0]
    col_block = tiles_ref[tile, 1]
    for s in range(SB):
        left_l = l_ref[row_block * SB + s]
        for u in range(SB):
            right_l = l_ref[col_block * SB + u]
            low = jnp.abs(left_l - right_l)
            high = jnp.minimum(left_l + right_l, orders - 1)
            count = jnp.maximum(high - low + 2, 0) // 2
            pair = s * SB + u

            def step(chunk, accum):
                scaled = []
                radials = []
                for inner in range(CHUNK):
                    number = chunk * CHUNK + inner
                    wanted = low + 2 * number
                    order = jnp.minimum(wanted, orders - 2 + (low & 1))
                    slot = order // 2
                    weight = jnp.where(number < count, angular_ref[0, order, pair], 0.0)
                    layer = jnp.concatenate(
                        [form_ref[part, slot][pair : pair + 1].astype(jnp.float32) for part in range(parts)], axis=1
                    )
                    factor = (layer * weight).astype(jnp.bfloat16)
                    radial = bessel_ref[order]
                    scaled.append(radial * factor)
                    radials.append(radial)
                scaled = jnp.concatenate(scaled, axis=1)
                radials = jnp.concatenate(radials, axis=1)
                if flip:
                    product = lax.dot_general(radials, scaled, NT_DIMS, preferred_element_type=jnp.float32)
                else:
                    product = lax.dot_general(scaled, radials, NT_DIMS, preferred_element_type=jnp.float32)
                return accum + product

            steps = (count + CHUNK - 1) // CHUNK
            accum = lax.fori_loop(0, steps, step, jnp.zeros((momenta, momenta), jnp.float32))
            row, col = (u, s) if flip else (s, u)
            out_ref[0, row * momenta : (row + 1) * momenta, col * momenta : (col + 1) * momenta] = accum.astype(
                out_ref.dtype
            )


def kernel_block(tile, tile_blocks, state_l, angular, form, bessel, flip):
    orders, momenta, radial = bessel.shape
    side = SB * momenta
    smem = pl.BlockSpec(memory_space=pltpu.SMEM)
    vmem = pl.BlockSpec(memory_space=pltpu.VMEM)
    return pl.pallas_call(
        functools.partial(block_kernel, flip),
        out_shape=jax.ShapeDtypeStruct((1, side, side), jnp.bfloat16),
        in_specs=[smem, smem, smem, smem, vmem, vmem],
        out_specs=vmem,
        compiler_params=pltpu.CompilerParams(vmem_limit_bytes=32 * 2**20),
        cost_estimate=pl.CostEstimate(
            flops=PAIRS * orders * momenta * momenta * radial, bytes_accessed=6 * 2**20, transcendentals=0
        ),
        name="lower_block" if flip else "upper_block",
    )(tile, tile_blocks, state_l, angular, form, bessel)


def from_partner(block, axis, apart):
    count = lax.axis_size(axis)
    route = []
    for low in range(count):
        high = low | 1 << apart
        if high != low and high < count:
            route += [(low, high), (high, low)]
    return lax.ppermute(block, axis, route)


def body(orbitals, kernel, bessel, angular, state_l, tile_blocks):
    pair_count = lax.axis_size("pair")
    rad_count = lax.axis_size("rad")
    tiles = tile_blocks.shape[0]
    tile = (lax.axis_index("pair") * rad_count + lax.axis_index("rad")).astype(jnp.int32)
    other = (tile + tiles // 2) % tiles
    top_bit = pair_count.bit_length() - 2
    angular_other = from_partner(angular, "pair", top_bit)
    partial = partial_form(orbitals, kernel, state_l, tile_blocks, pair_count, rad_count)
    summed = lax.psum_scatter(partial, "pair", scatter_dimension=0, tiled=False)
    form = lax.all_to_all(summed, "rad", split_axis=0, concat_axis=0, tiled=True)
    form_other = from_partner(form, "pair", top_bit)
    upper = kernel_block(tile[None], tile_blocks, state_l, angular, form, bessel, False)
    lower = kernel_block(other[None], tile_blocks, state_l, angular_other, form_other, bessel, True)
    return (upper, lower)


def solution(mesh):
    in_specs = (P(), P(None, "rad", "pair"), P(), P(("pair", "rad"), None, None), P(), P())
    out_specs = (P(("pair", "rad"), None, None), P(("pair", "rad"), None, None))
    return jax.shard_map(body, mesh=mesh, in_specs=in_specs, out_specs=out_specs, check_vma=False)
```

time: 242 us -> 125 us (0.52)
  the two profiles are of different devices: /device:TPU:0 before, /device:TPU:5 now
where the time goes in v1:
time: 125 us
  waiting for transfers between devices  66.8 us (53%)
  Pallas kernels  28.8 us (23%)
  between operations  14.1 us (11%)
  starting transfers between devices  8.83 us (7%)
  local copies, waits for them, and re-layouts  5.34 us (4%)
    reduce_scatter x1, waiting for transfers between devices, body(): summed = lax.psum_scatter(partial, 'pair', scatter_dimension=0, tiled=False)  63.9 us
    pallas_call x2, Pallas kernels, kernel_block(): pl.pallas_call(functools.partial(block_kernel, flip), out_shape=jax.Shape...  25.4 us
    all_to_all x1, starting transfers between devices, body(): lax.all_to_all(summed, 'rad', split_axis=0, concat_axis=0, tiled=True)  5.9 us
    unnamed x16, local copies, waits for them, and re-layouts  5.02 us
    pallas_call x1, Pallas kernels, partial_form(): pl.pallas_call(partial_form_kernel, grid=(pair_count // groups,), out_sha...  3.36 us
    all_to_all x1, waiting for transfers between devices, body(): lax.all_to_all(summed, 'rad', split_axis=0, concat_axis=0, tiled=True)  2.93 us
    ppermute x2, starting transfers between devices, from_partner(): return lax.ppermute(block, axis, route)  2.89 us
  transfers between devices with their start and end apart: 4, of which 2 were waited for; matrix products, arithmetic and copies ran while one was open for 0% of the time, Pallas kernels for 10%

profile of v1, /device:TPU:5, one launch (start us, length us, event | category | flops | bytes accessed | tf_op | source)
XLA Modules:
  0.0 124.7 jit_solution(15251035173832209784)
XLA Ops:
  7.2 0.0 reduce-scatter.2.cloned.1.call-start
  7.2 0.8 multiply_bitcast_fusion
  8.0 0.1 broadcast_add_fusion
  8.1 0.2 add.93.rows_ref
  8.2 0.0 copy-start.5
  8.2 0.0 copy-start.6
  8.3 0.0 copy-start.3
  8.3 0.2 add.94.cols_ref
  8.4 0.0 copy-start
  8.4 1.2 copy-done
  9.7 0.0 copy-start.1
  9.7 1.1 copy-done.1
  10.8 0.0 copy-start.2
  10.8 0.7 copy-done.2
  11.5 3.4 %partial_form.1 = bf16[8,4,6,16,256]{4,3,2,1,0:T(8,128)(2,1)} custom-call(s32[512,1]{1,0:T(8,128)S(1)} %add.93.rows_ref, s32[512,1]{1,0:T(8,128)S(1)} %add.94.cols_ref, s32[1,500]{1,0:T(1,128)S(1)} %bitcast.8, bf16[500,1024]{1,0:T(8,128)(2,1)S(1)} %copy-done, bf16[12,256,128]{2,1,0:T(8,128)(2,1)S(1)} %copy-done.1), custom_call_target="tpu_custom_call" | custom-call | flops 402653184 | bytes 4194304 | tf_op jit(solution)/shard_map/partial_form/pallas_call | solution.py:56
  14.8 0.0 reduce-scatter.2.cloned.1.call-update
  14.9 63.9 %reduce-scatter.2.cloned.1.call-done = bf16[1,4,6,16,256]{4,3,2,1,0:T(8,128)(2,1)} async-done(((bf16[8,4,6,16,256]{4,3,2,1,0:T(8,128)(2,1)}), bf16[1,4,6,16,256]{4,3,2,1,0:T(8,128)(2,1)}) %reduce-scatter.2.cloned.1.call-update) | async-done | bytes 196624 | tf_op jit(solution)/shard_map/reduce_scatter | solution.py:160
  78.7 5.9 %all-to-all-start = ((bf16[4,6,16,256]{3,2,1,0:T(8,128)(2,1)}), bf16[4,6,16,256]{3,2,1,0:T(8,128)(2,1)S(1)}, u32[]{:S(2)}, u32[]{:S(2)}) async-start(bf16[4,6,16,256]{3,2,1,0:T(8,128)(2,1)} %bitcast.9), calls=%async_computation.1 | async-start | bytes 393216 | tf_op jit(solution)/shard_map/all_to_all | solution.py:161
  84.6 0.0 copy-done.5
  84.6 1.4 %collective-permute-start = (f32[1,12,16]{2,1,0:T(8,128)S(1)}, f32[1,12,16]{2,1,0:T(8,128)S(1)}, u32[]{:S(2)}, u32[]{:S(2)}) collective-permute-start(f32[1,12,16]{2,1,0:T(8,128)S(1)} %copy.15.angular_ref), channel_id=1, source_target_pairs={{0,16},{16,0},{4,20},{20,4},{8,24},{24,8},{12,28},{28,12},{1,17},{... | collective-permute-start | bytes 2312 | tf_op jit(solution)/shard_map/ppermute | solution.py:148
  86.1 0.0 copy-done.6
  86.1 0.1 copy.14.tiles_ref
  86.2 2.9 %all-to-all-done.form_ref = bf16[4,6,16,256]{3,2,1,0:T(8,128)(2,1)S(1)} async-done(((bf16[4,6,16,256]{3,2,1,0:T(8,128)(2,1)}), bf16[4,6,16,256]{3,2,1,0:T(8,128)(2,1)S(1)}, u32[]{:S(2)}, u32[]{:S(2)}) %all-to-all-start) | async-done | bytes 196640 | tf_op jit(solution)/shard_map/all_to_all | solution.py:161
  89.1 1.4 %collective-permute-start.1 = (bf16[4,6,16,256]{3,2,1,0:T(8,128)(2,1)S(1)}, bf16[4,6,16,256]{3,2,1,0:T(8,128)(2,1)S(1)}, u32[]{:S(2)}, u32[]{:S(2)}) collective-permute-start(bf16[4,6,16,256]{3,2,1,0:T(8,128)(2,1)S(1)} %all-to-all-done.form_ref), channel_id=1, source_target_pairs={{0,16},{16,0},{4,20},{20,4},{8,24},{24,8},{12,28},{28,12},{1,17},{... | collective-permute-start | bytes 589832 | tf_op jit(solution)/shard_map/ppermute | solution.py:148
  90.5 0.0 copy-done.3
  90.6 0.0 copy-start.4
  90.6 1.9 %copy-done.4 = bf16[12,128,1024]{2,1,0:T(8,128)(2,1)S(1)} copy-done((bf16[12,128,1024]{2,1,0:T(8,128)(2,1)S(1)}, bf16[12,128,1024]{2,1,0:T(8,128)(2,1)}, u32[]{:S(2)}) %copy-start.4) | copy-done | bytes 3145752
  92.4 12.4 %upper_block.1 = bf16[1,512,512]{2,1,0:T(8,128)(2,1)} custom-call(s32[1]{0:T(128)} %bitcast.tile_ref, s32[32,2]{1,0:T(8,128)S(1)} %copy.14.tiles_ref, s32[500]{0:T(512)S(1)} %copy-done.3, f32[1,12,16]{2,1,0:T(8,128)S(1)} %copy.15.angular_ref, bf16[4,6,16,256]{3,2,1,0:T(8,128)(2,1)S(1)} %all-to-all-done.form_ref, bf16[12,128,1024]{2,1,0:T(8,128)(2,1)S(1)} %copy-done.4), custom_call_target="tpu_custom_call" | custom-call | flops 3221225472 | bytes 6291456 | tf_op jit(solution)/shard_map/upper_block/pallas_call | solution.py:128
  104.9 0.0 collective-permute-done.angular_ref
  104.9 0.0 collective-permute-done.1.form_ref
  104.9 13.0 %lower_block.1 = bf16[1,512,512]{2,1,0:T(8,128)(2,1)} custom-call(s32[1]{0:T(128)} %bitcast.5.tile_ref, s32[32,2]{1,0:T(8,128)S(1)} %copy.14.tiles_ref, s32[500]{0:T(512)S(1)} %copy-done.3, f32[1,12,16]{2,1,0:T(8,128)S(1)} %collective-permute-done.angular_ref, bf16[4,6,16,256]{3,2,1,0:T(8,128)(2,1)S(1)} %collective-permute-done.1.form_ref, ...), custom_call_target="tpu_custom_call" | custom-call | flops 3221225472 | bytes 6291456 | tf_op jit(solution)/shard_map/lower_block/pallas_call | solution.py:128
  (3 shorter events, 0.0 us)
Async XLA Ops:
  7.2 71.6 %reduce-scatter.2.cloned.1.call-start = ((), (), s32[]{:S(2)}) async-start(), calls=%async_computation.2 | async-start | bytes 1769472 | tf_op jit(solution)/shard_map/reduce_scatter | solution.py:160
  8.2 76.4 %copy-start.5 = (f32[1,12,16]{2,0,1:T(1,128)S(1)}, f32[1,12,16]{2,0,1:T(1,128)}, u32[]{:S(2)}) copy-start(f32[1,12,16]{2,0,1:T(1,128)} %param.9) | copy-start | bytes 2308
  8.2 77.8 %copy-start.6 = (s32[32,2]{0,1:T(2,128)S(1)}, s32[32,2]{0,1:T(2,128)}, u32[]{:S(2)}) copy-start(s32[32,2]{0,1:T(2,128)} %param.11) | copy-start | bytes 772
  8.3 82.3 %copy-start.3 = (s32[500]{0:T(512)S(1)}, s32[500]{0:T(512)}, u32[]{:S(2)}) copy-start(s32[500]{0:T(512)} %l_ref.3) | copy-start | bytes 6004
  8.4 1.2 copy-start
  9.7 1.1 copy-start.1
  10.8 0.7 copy-start.2
  78.7 10.4 %all-to-all-start = ((bf16[4,6,16,256]{3,2,1,0:T(8,128)(2,1)}), bf16[4,6,16,256]{3,2,1,0:T(8,128)(2,1)S(1)}, u32[]{:S(2)}, u32[]{:S(2)}) async-start(bf16[4,6,16,256]{3,2,1,0:T(8,128)(2,1)} %bitcast.9), calls=%async_computation.1 | async-start | bytes 393216 | tf_op jit(solution)/shard_map/all_to_all | solution.py:161
  84.6 20.2 %collective-permute-start = (f32[1,12,16]{2,1,0:T(8,128)S(1)}, f32[1,12,16]{2,1,0:T(8,128)S(1)}, u32[]{:S(2)}, u32[]{:S(2)}) collective-permute-start(f32[1,12,16]{2,1,0:T(8,128)S(1)} %copy.15.angular_ref), channel_id=1, source_target_pairs={{0,16},{16,0},{4,20},{20,4},{8,24},{24,8},{12,28},{28,12},{1,17},{... | collective-permute-start | bytes 2312 | tf_op jit(solution)/shard_map/ppermute | solution.py:148
  89.1 15.8 %collective-permute-start.1 = (bf16[4,6,16,256]{3,2,1,0:T(8,128)(2,1)S(1)}, bf16[4,6,16,256]{3,2,1,0:T(8,128)(2,1)S(1)}, u32[]{:S(2)}, u32[]{:S(2)}) collective-permute-start(bf16[4,6,16,256]{3,2,1,0:T(8,128)(2,1)S(1)} %all-to-all-done.form_ref), channel_id=1, source_target_pairs={{0,16},{16,0},{4,20},{20,4},{8,24},{24,8},{12,28},{28,12},{1,17},{... | collective-permute-start | bytes 589832 | tf_op jit(solution)/shard_map/ppermute | solution.py:148
  90.6 1.9 %copy-start.4 = (bf16[12,128,1024]{2,1,0:T(8,128)(2,1)S(1)}, bf16[12,128,1024]{2,1,0:T(8,128)(2,1)}, u32[]{:S(2)}) copy-start(bf16[12,128,1024]{2,1,0:T(8,128)(2,1)} %bessel_ref.3) | copy-start | bytes 9437188
Sparse Core Ops, SparseCore 0:
  15.0 63.6 reduce-scatter.1

commit v2 on v1

--- a/solution.py
+++ b/solution.py
@@ -10,67 +10,186 @@
 SB = 4
 PAIRS = SB * SB
 CHUNK = 2
+OUTER = 4
 NT_DIMS = (((1,), (1,)), ((), ()))
 
 
-def partial_form_kernel(rows_ref, cols_ref, l_ref, orb_ref, kernel_ref, out_ref):
-    groups, members, slots = out_ref.shape[:3]
-    count = rows_ref.shape[0]
+def opposite(value, bits):
+    if bits == 1:
+        return value + 1 - 2 * lax.rem(value, 2)
+    if bits == 2:
+        return lax.rem(value + 2, OUTER)
+    return OUTER - 1 - value
+
+
+STAGES = (2, 3, 1, 0)
+
+
+def form_kernel(
+    rows_ref, cols_ref, l_ref, orb_ref, kernel_ref, out_ref,
+    part, inner_in, outer_out, outer_in, whole, landed,
+    inner_send, inner_recv, outer_send, outer_recv, rad_send, rad_recv,
+):
+    inner_count, members, slots = part.shape[1:4]
     states = orb_ref.shape[0]
-    ids = lax.broadcasted_iota(jnp.int32, (count, states), 1)
-    left_hot = ids == rows_ref[...]
-    right_hot = ids == cols_ref[...]
+    block = inner_count * members * PAIRS
+    pair = lax.axis_index("pair")
+    rad = lax.axis_index("rad")
+    outer, inner = pair // inner_count, lax.rem(pair, inner_count)
+
+    def device(outer_at, inner_at, rad_at):
+        return (outer_at * inner_count + inner_at, rad_at)
+
+    peers = [device(outer, opposite(inner, j), rad) for j in range(1, inner_count)]
+    peers += [device(opposite(outer, k), inner, rad) for k in range(1, OUTER)]
+    peers += [device(outer, inner, lax.rem(rad + m, members)) for m in range(1, members)]
+    barrier = pltpu.get_barrier_semaphore()
+    for peer in peers:
+        pl.semaphore_signal(barrier, inc=1, device_id=peer, device_id_type=pl.DeviceIdType.MESH)
+
     levels = l_ref[...].astype(jnp.float32)
 
-    def pick(hot):
+    def pick(ids_ref, start):
+        ids = ids_ref[pl.ds(start, block), :]
+        hot = lax.broadcasted_iota(jnp.int32, (block, states), 1) == ids
         value = jnp.dot(
             jnp.where(hot, 1.0, 0.0).astype(jnp.bfloat16), orb_ref[...], preferred_element_type=jnp.float32
         )
         level = jnp.sum(jnp.where(hot, levels, 0.0), axis=1, keepdims=True)
         return value, level
 
-    left, left_l = pick(left_hot)
-    right, right_l = pick(right_hot)
-    density = (left * right).astype(jnp.bfloat16)
-    odd = ((left_l + right_l).astype(jnp.int32) & 1) == 1
-    for slot in range(slots):
-        even_form = lax.dot_general(density, kernel_ref[2 * slot], NT_DIMS, preferred_element_type=jnp.float32)
-        odd_form = lax.dot_general(density, kernel_ref[2 * slot + 1], NT_DIMS, preferred_element_type=jnp.float32)
-        form = jnp.where(odd, odd_form, even_form).astype(jnp.bfloat16)
-        form = form.reshape(groups, members, PAIRS, form.shape[-1])
-        for group in range(groups):
-            for member in range(members):
-                out_ref[group, member, slot] = form[group, member]
-
-
-def partial_form(orbitals, kernel, state_l, tile_blocks, pair_count, rad_count):
+    def partial_sums(stage, target):
+        start = pl.multiple_of(target * block, block)
+        left, left_l = pick(rows_ref, start)
+        right, right_l = pick(cols_ref, start)
+        density = (left * right).astype(jnp.bfloat16)
+        total_l = left_l + right_l
+        odd = total_l - 2.0 * jnp.floor(total_l * 0.5) > 0.5
+        for slot in range(slots):
+            even_form = lax.dot_general(density, kernel_ref[2 * slot], NT_DIMS, preferred_element_type=jnp.float32)
+            odd_form = lax.dot_general(density, kernel_ref[2 * slot + 1], NT_DIMS, preferred_element_type=jnp.float32)
+            form = jnp.where(odd, odd_form, even_form).astype(jnp.bfloat16)
+            form = form.reshape(inner_count, members, PAIRS, form.shape[-1])
+            for at in range(inner_count):
+                for member in range(members):
+                    part[stage, at, member, slot] = form[at, member]
+
+    inner_copies = []
+    for stage in STAGES:
+        partial_sums(stage, outer if stage == 0 else opposite(outer, stage))
+        if stage == STAGES[0]:
+            pl.semaphore_wait(barrier, len(peers))
+        for j in range(1, inner_count):
+            there = opposite(inner, j)
+            copy = pltpu.make_async_remote_copy(
+                src_ref=part.at[stage, there],
+                dst_ref=inner_in.at[stage, j - 1],
+                send_sem=inner_send.at[stage, j - 1],
+                recv_sem=inner_recv.at[stage, j - 1],
+                device_id=device(outer, there, rad),
+                device_id_type=pl.DeviceIdType.MESH,
+            )
+            copy.start()
+            inner_copies.append((stage, copy))
+
+    outer_copies = []
+    total = None
+    for stage in STAGES:
+        for at, copy in inner_copies:
+            if at == stage:
+                copy.wait_recv()
+        for member in range(members):
+            summed = part[stage, inner, member].astype(jnp.float32)
+            for j in range(1, inner_count):
+                summed += inner_in[stage, j - 1, member].astype(jnp.float32)
+            if stage:
+                outer_out[stage - 1, member] = summed.astype(jnp.bfloat16)
+            else:
+                whole[member] = summed
+        if stage:
+            copy = pltpu.make_async_remote_copy(
+                src_ref=outer_out.at[stage - 1],
+                dst_ref=outer_in.at[stage - 1],
+                send_sem=outer_send.at[stage - 1],
+                recv_sem=outer_recv.at[stage - 1],
+                device_id=device(opposite(outer, stage), inner, rad),
+                device_id_type=pl.DeviceIdType.MESH,
+            )
+            copy.start()
+            outer_copies.append(copy)
+
+    for copy in outer_copies:
+        copy.wait_recv()
+    rad_copies = []
+    for m in [*range(1, members), 0]:
+        there = lax.rem(rad + m, members)
+        summed = whole[there]
+        for stage in range(1, OUTER):
+            summed += outer_in[stage - 1, there].astype(jnp.float32)
+        if m:
+            outbox = landed.at[0, m]
+            landed[0, m] = summed.astype(jnp.bfloat16)
+            copy = pltpu.make_async_remote_copy(
+                src_ref=outbox,
+                dst_ref=landed.at[1, rad],
+                send_sem=rad_send.at[m - 1],
+                recv_sem=rad_recv.at[m - 1],
+                device_id=device(outer, inner, there),
+                device_id_type=pl.DeviceIdType.MESH,
+            )
+            copy.start()
+            rad_copies.append(copy)
+        else:
+            out_ref[rad] = summed.astype(jnp.bfloat16)
+    for m, copy in enumerate(rad_copies, 1):
+        copy.wait_recv()
+        source = lax.rem(rad + members - m, members)
+        out_ref[source] = landed[1, source]
+    for at, copy in inner_copies:
+        copy.wait_send()
+    for copy in outer_copies + rad_copies:
+        copy.wait_send()
+
+
+def form_of_tile(orbitals, kernel, state_l, tile_blocks, pair_count, rad_count):
     tiles = tile_blocks.shape[0]
     states = orbitals.shape[0]
     orders, radial, depth = kernel.shape
     place = jnp.arange(PAIRS, dtype=jnp.int32)[None]
     rows = (tile_blocks[:, 0:1] * SB + place // SB).reshape(tiles * PAIRS, 1)
     cols = (tile_blocks[:, 1:2] * SB + place % SB).reshape(tiles * PAIRS, 1)
-    members = tiles // pair_count
-    groups = 2
-    block = groups * members * PAIRS
+    inner_count = pair_count // OUTER
+    piece = (orders // 2, PAIRS, radial)
+    own = lax.dynamic_slice_in_dim(orbitals, lax.axis_index("pair") * depth, depth, 1)
+    vmem = pl.BlockSpec(memory_space=pltpu.VMEM)
+    dma = pltpu.SemaphoreType.DMA
     return pl.pallas_call(
-        partial_form_kernel,
-        grid=(pair_count // groups,),
-        out_shape=jax.ShapeDtypeStruct((pair_count, members, orders // 2, PAIRS, radial), jnp.bfloat16),
-        in_specs=[
-            pl.BlockSpec((block, 1), lambda i: (i, 0)),
-            pl.BlockSpec((block, 1), lambda i: (i, 0)),
-            pl.BlockSpec((1, states), lambda i: (0, 0)),
-            pl.BlockSpec((states, depth), lambda i: (0, lax.axis_index("pair"))),
-            pl.BlockSpec((orders, radial, depth), lambda i: (0, 0, 0)),
+        form_kernel,
+        out_shape=jax.ShapeDtypeStruct((rad_count, *piece), jnp.bfloat16),
+        in_specs=[vmem] * 5,
+        out_specs=vmem,
+        scratch_shapes=[
+            pltpu.VMEM((OUTER, inner_count, rad_count, *piece), jnp.bfloat16),
+            pltpu.VMEM((OUTER, inner_count - 1, rad_count, *piece), jnp.bfloat16),
+            pltpu.VMEM((OUTER - 1, rad_count, *piece), jnp.bfloat16),
+            pltpu.VMEM((OUTER - 1, rad_count, *piece), jnp.bfloat16),
+            pltpu.VMEM((rad_count, *piece), jnp.float32),
+            pltpu.VMEM((2, rad_count, *piece), jnp.bfloat16),
+            dma((OUTER, inner_count - 1)),
+            dma((OUTER, inner_count - 1)),
+            dma((OUTER - 1,)),
+            dma((OUTER - 1,)),
+            dma((rad_count - 1,)),
+            dma((rad_count - 1,)),
         ],
-        out_specs=pl.BlockSpec((groups, members, orders // 2, PAIRS, radial), lambda i: (i, 0, 0, 0, 0)),
-        compiler_params=pltpu.CompilerParams(vmem_limit_bytes=32 * 2**20),
+        compiler_params=pltpu.CompilerParams(
+            vmem_limit_bytes=40 * 2**20, collective_id=0, has_side_effects=True
+        ),
         cost_estimate=pl.CostEstimate(
             flops=2 * tiles * PAIRS * orders * radial * depth, bytes_accessed=4 * 2**20, transcendentals=0
         ),
-        name="partial_form",
-    )(rows, cols, state_l.reshape(1, states), orbitals, kernel)
+        name="form_of_tile",
+    )(rows, cols, state_l.reshape(1, states), own, kernel)
 
 
 def block_kernel(flip, tile_ref, tiles_ref, l_ref, angular_ref, form_ref, bessel_ref, out_ref):
@@ -156,9 +275,7 @@
     other = (tile + tiles // 2) % tiles
     top_bit = pair_count.bit_length() - 2
     angular_other = from_partner(angular, "pair", top_bit)
-    partial = partial_form(orbitals, kernel, state_l, tile_blocks, pair_count, rad_count)
-    summed = lax.psum_scatter(partial, "pair", scatter_dimension=0, tiled=False)
-    form = lax.all_to_all(summed, "rad", split_axis=0, concat_axis=0, tiled=True)
+    form = form_of_tile(orbitals, kernel, state_l, tile_blocks, pair_count, rad_count)
     form_other = from_partner(form, "pair", top_bit)
     upper = kernel_block(tile[None], tile_blocks, state_l, angular, form, bessel, False)
     lower = kernel_block(other[None], tile_blocks, state_l, angular_other, form_other, bessel, True)

time: 125 us -> 69.7 us (0.56)
  the two profiles are of different devices: /device:TPU:5 before, /device:TPU:2 now
where the time goes in v2:
time: 69.7 us; the launch traced here: 70.8 us
  Pallas kernels  54.9 us (79%)
  local copies, waits for them, and re-layouts  8.18 us (12%)
  starting transfers between devices  6.14 us (9%)
  other arithmetic  0.84 us (1%)
  between operations  0.71 us (1%)
    pallas_call x1, Pallas kernels, form_of_tile(): pl.pallas_call(form_kernel, out_shape=jax.ShapeDtypeStruct((rad_count, *p...  28.2 us
    pallas_call x2, Pallas kernels, kernel_block(): pl.pallas_call(functools.partial(block_kernel, flip), out_shape=jax.Shape...  26.7 us
    unnamed x16, local copies, waits for them, and re-layouts  7.82 us
    ppermute x2, starting transfers between devices, from_partner(): return lax.ppermute(block, axis, route)  6.14 us
  transfers between devices with their start and end apart: 2, of which 0 were waited for; matrix products, arithmetic and copies ran while one was open for 3% of the time, Pallas kernels for 57%

profile of v2, /device:TPU:2, one launch (start us, length us, event | category | flops | bytes accessed | tf_op | source)
XLA Modules:
  0.0 70.8 jit_solution(10466445526170935087)
XLA Ops:
  0.6 0.0 copy-start
  0.6 0.8 %copy.15.angular_ref = f32[1,12,16]{2,1,0:T(8,128)S(1)} copy(f32[1,12,16]{2,0,1:T(1,128)} %param.9) | data formatting | bytes 1536 | tf_op args[3]
  1.4 2.6 %collective-permute-start = (f32[1,12,16]{2,1,0:T(8,128)S(1)}, f32[1,12,16]{2,1,0:T(8,128)S(1)}, u32[]{:S(2)}, u32[]{:S(2)}) collective-permute-start(f32[1,12,16]{2,1,0:T(8,128)S(1)} %copy.15.angular_ref), channel_id=1, source_target_pairs={{0,16},{16,0},{4,20},{20,4},{8,24},{24,8},{12,28},{28,12},{1,17},{... | collective-permute-start | bytes 2312 | tf_op jit(solution)/shard_map/ppermute | solution.py:267
  4.0 0.8 %multiply_bitcast_fusion = (s32[32]{0:T(128)S(1)}, s32[32]{0:T(128)S(1)}) fusion(s32[32,2]{0,1:T(2,128)} %param.11), kind=kLoop, calls=%fused_computation.7 | loop fusion | flops 64 | bytes 512 | tf_op jit(solution)/shard_map/add | solution.py:160
  4.8 0.1 broadcast_add_fusion
  4.9 0.2 add.96.cols_ref
  5.0 0.2 add.95.rows_ref
  5.2 0.0 copy-done
  5.3 0.0 copy-start.1
  5.3 1.1 %copy-done.1 = bf16[12,256,128]{2,1,0:T(8,128)(2,1)S(1)} copy-done((bf16[12,256,128]{2,1,0:T(8,128)(2,1)S(1)}, bf16[12,256,128]{2,1,0:T(8,128)(2,1)}, u32[]{:S(2)}) %copy-start.1) | copy-done | bytes 786456
  6.4 0.0 copy-start.2
  6.4 0.7 copy-done.2
  7.1 28.2 %form_of_tile.1.form_ref = bf16[4,6,16,256]{3,2,1,0:T(8,128)(2,1)S(1)} custom-call(s32[512,1]{1,0:T(8,128)S(1)} %add.95.rows_ref, s32[512,1]{1,0:T(8,128)S(1)} %add.96.cols_ref, s32[1,500]{1,0:T(1,128)S(1)} %bitcast.7, bf16[500,128]{1,0:T(8,128)(2,1)S(1)} %constant_dynamic-slice_fusion.orb_ref, bf16[12,256,128]{2,1,0:T(8,128)(2,1)S(1)} %copy-done.1), custom_call_target="tpu_custom_call" | custom-call | flops 402653184 | bytes 4194304 | tf_op jit(solution)/shard_map/form_of_tile/pallas_call | solution.py:166
  35.3 3.6 %collective-permute-start.1 = (bf16[4,6,16,256]{3,2,1,0:T(8,128)(2,1)S(1)}, bf16[4,6,16,256]{3,2,1,0:T(8,128)(2,1)S(1)}, u32[]{:S(2)}, u32[]{:S(2)}) collective-permute-start(bf16[4,6,16,256]{3,2,1,0:T(8,128)(2,1)S(1)} %form_of_tile.1.form_ref), channel_id=1, source_target_pairs={{0,16},{16,0},{4,20},{20,4},{8,24},{24,8},{12,28},{28,12},{1,17},{... | collective-permute-start | bytes 589832 | tf_op jit(solution)/shard_map/ppermute | solution.py:267
  38.8 0.8 %copy.14.tiles_ref = s32[32,2]{1,0:T(8,128)S(1)} copy(s32[32,2]{0,1:T(2,128)} %param.11) | data formatting | bytes 512 | tf_op args[5]
  39.6 0.0 copy-start.3
  39.6 0.7 copy-done.3
  40.3 0.0 copy-start.5
  40.3 1.9 %copy-done.5 = bf16[12,128,1024]{2,1,0:T(8,128)(2,1)S(1)} copy-done((bf16[12,128,1024]{2,1,0:T(8,128)(2,1)S(1)}, bf16[12,128,1024]{2,1,0:T(8,128)(2,1)}, u32[]{:S(2)}) %copy-start.5) | copy-done | bytes 3145752
  42.2 0.0 copy-start.4
  42.2 12.5 %upper_block.1 = bf16[1,512,512]{2,1,0:T(8,128)(2,1)} custom-call(s32[1]{0:T(128)} %bitcast.tile_ref, s32[32,2]{1,0:T(8,128)S(1)} %copy.14.tiles_ref, s32[500]{0:T(512)S(1)} %copy-done.3, f32[1,12,16]{2,1,0:T(8,128)S(1)} %copy.15.angular_ref, bf16[4,6,16,256]{3,2,1,0:T(8,128)(2,1)S(1)} %form_of_tile.1.form_ref, bf16[12,128,1024]{2,1,0:T(8,128)(2,1)S(1)} %copy-done.5), custom_call_target="tpu_custom_call" | custom-call | flops 3221225472 | bytes 6291456 | tf_op jit(solution)/shard_map/upper_block/pallas_call | solution.py:247
  54.6 0.0 collective-permute-done.angular_ref
  54.6 0.0 collective-permute-done.1.form_ref
  54.6 0.0 copy-done.4
  54.6 0.0 copy-start.6
  54.7 1.9 %copy-done.6 = bf16[12,128,1024]{2,1,0:T(8,128)(2,1)S(1)} copy-done((bf16[12,128,1024]{2,1,0:T(8,128)(2,1)S(1)}, bf16[12,128,1024]{2,1,0:T(8,128)(2,1)}, u32[]{:S(2)}) %copy-start.6) | copy-done | bytes 3145752
  56.5 14.2 %lower_block.1 = bf16[1,512,512]{2,1,0:T(8,128)(2,1)} custom-call(s32[1]{0:T(128)} %bitcast.4.tile_ref, s32[32,2]{1,0:T(8,128)S(1)} %copy.14.tiles_ref, s32[500]{0:T(512)S(1)} %copy-done.4, f32[1,12,16]{2,1,0:T(8,128)S(1)} %collective-permute-done.angular_ref, bf16[4,6,16,256]{3,2,1,0:T(8,128)(2,1)S(1)} %collective-permute-done.1.form_ref, ...), custom_call_target="tpu_custom_call" | custom-call | flops 3221225472 | bytes 6291456 | tf_op jit(solution)/shard_map/lower_block/pallas_call | solution.py:247
  (3 shorter events, 0.1 us)
Async XLA Ops:
  0.6 4.6 %copy-start = (bf16[500,1024]{1,0:T(8,128)(2,1)S(1)}, bf16[500,1024]{1,0:T(8,128)(2,1)}, u32[]{:S(2)}) copy-start(bf16[500,1024]{1,0:T(8,128)(2,1)} %param.6) | copy-start | bytes 3072004
  1.4 53.2 %collective-permute-start = (f32[1,12,16]{2,1,0:T(8,128)S(1)}, f32[1,12,16]{2,1,0:T(8,128)S(1)}, u32[]{:S(2)}, u32[]{:S(2)}) collective-permute-start(f32[1,12,16]{2,1,0:T(8,128)S(1)} %copy.15.angular_ref), channel_id=1, source_target_pairs={{0,16},{16,0},{4,20},{20,4},{8,24},{24,8},{12,28},{28,12},{1,17},{... | collective-permute-start | bytes 2312 | tf_op jit(solution)/shard_map/ppermute | solution.py:267
  5.3 1.1 %copy-start.1 = (bf16[12,256,128]{2,1,0:T(8,128)(2,1)S(1)}, bf16[12,256,128]{2,1,0:T(8,128)(2,1)}, u32[]{:S(2)}) copy-start(bf16[12,256,128]{2,1,0:T(8,128)(2,1)} %kernel_ref.1) | copy-start | bytes 2359300
  6.4 0.7 copy-start.2
  35.3 19.4 %collective-permute-start.1 = (bf16[4,6,16,256]{3,2,1,0:T(8,128)(2,1)S(1)}, bf16[4,6,16,256]{3,2,1,0:T(8,128)(2,1)S(1)}, u32[]{:S(2)}, u32[]{:S(2)}) collective-permute-start(bf16[4,6,16,256]{3,2,1,0:T(8,128)(2,1)S(1)} %form_of_tile.1.form_ref), channel_id=1, source_target_pairs={{0,16},{16,0},{4,20},{20,4},{8,24},{24,8},{12,28},{28,12},{1,17},{... | collective-permute-start | bytes 589832 | tf_op jit(solution)/shard_map/ppermute | solution.py:267
  39.6 0.7 copy-start.3
  40.3 1.9 %copy-start.5 = (bf16[12,128,1024]{2,1,0:T(8,128)(2,1)S(1)}, bf16[12,128,1024]{2,1,0:T(8,128)(2,1)}, u32[]{:S(2)}) copy-start(bf16[12,128,1024]{2,1,0:T(8,128)(2,1)} %bessel_ref.3) | copy-start | bytes 9437188
  42.2 12.5 %copy-start.4 = (s32[500]{0:T(512)S(1)}, s32[500]{0:T(512)}, u32[]{:S(2)}) copy-start(s32[500]{0:T(512)} %l_ref.3) | copy-start | bytes 6004
  54.6 1.9 %copy-start.6 = (bf16[12,128,1024]{2,1,0:T(8,128)(2,1)S(1)}, bf16[12,128,1024]{2,1,0:T(8,128)(2,1)}, u32[]{:S(2)}) copy-start(bf16[12,128,1024]{2,1,0:T(8,128)(2,1)} %bessel_ref.3) | copy-start | bytes 9437188
